TPU v7x, 32 devices: a whole 2x2x4 slice. The times are simulated.
32 devices in a mesh: section: 4 (over y, x), shard: 8 (over z, core).
Axes of the slice: x: 2, y: 2, z: 4, core: 2. Of those that a mesh axis runs over, the one named last changes fastest.
Arguments:
- section_inputs: bfloat16 [4, 2, 384, 16384], P('section', None, None, 'shard'), may hold values from -12 to 12
- top_grad: bfloat16 [2, 384, 16384], P(None, None, 'shard'), may hold values from -6 to 6
- norm_gain: float32 [4, 16384], P('section', 'shard'), may hold values from 0.1 to 1.9
- key_grad: bfloat16 [4, 2, 384, 512], P('section'), may hold values from -18 to 18
- value_grad: bfloat16 [4, 2, 384, 512], P('section'), may hold values from -6 to 6
- key_weight: bfloat16 [4, 512, 16384], P('section', None, 'shard'), may hold values from -0.046875 to 0.046875
- value_weight: bfloat16 [4, 512, 16384], P('section', None, 'shard'), may hold values from -0.046875 to 0.046875
- first_codes: int32 [4, 2, 512, 16384], P('section', None, None, 'shard'), may hold values from 0 to 15
- second_codes: int32 [4, 2, 512, 16384], P('section', None, None, 'shard'), may hold values from 0 to 15
- first_scale: float32 [4, 2, 512, 128], P('section', None, None, 'shard'), may hold values from 2.4414063e-05 to 0.00024414062
- second_scale: float32 [4, 2, 512, 128], P('section', None, None, 'shard'), may hold values from 1.4901161e-09 to 1.4901161e-08
Outputs:
- direction: float32 [4, 2, 512, 16384], P('section', None, None, 'shard')
- first_ratio: float32 [4, 2, 512, 16384], P('section', None, None, 'shard')
- second_ratio: float32 [4, 2, 512, 16384], P('section', None, None, 'shard')
- leaving: bfloat16 [4, 2, 384, 16384], P('section', None, None, 'shard')
Inputs may be any that keep to these rules, and one draw needn't show every extreme that they name: `first_codes`: codes follow the encoding of the steps.
All inputs are finite; a program needn't handle non-finite values. Where the computation divides by a largest or mean magnitude, that divisor is 1e-20 or more.
Results may differ from a plain program's by a relative error of at most 0.0085.
The roundings to bfloat16 on the way count: a program that leaves them out, or rounds other values in their place, can miss the bound.
Values may be sent and summed in bfloat16 or wider, within the bound.
A program may use at most 128 MiB of HBM per device.

v0:
```python
import jax
import jax.numpy as jnp
from jax import lax
from jax.sharding import PartitionSpec as P

D = 16384
QB = 128
STEP = 20


beta_one = 0.9
beta_two = 0.95
clip_norm = 1.0


def optimizer(gradients, square_total, first_codes, second_codes, first_scale, second_scale):
    clip_factor = jnp.minimum(1.0, clip_norm / (jnp.sqrt(square_total) + 1e-06))
    clipped = clip_factor * gradients
    sign_part = 1.0 - 2.0 * (first_codes // 8).astype(jnp.float32)
    first_old = (
        jnp.repeat(first_scale, QB, axis=-1)
        * sign_part
        * jnp.exp2(-(first_codes % 8).astype(jnp.float32))
    )
    second_old = jnp.repeat(second_scale, QB, axis=-1) * jnp.exp2(-second_codes.astype(jnp.float32))
    first_new = beta_one * first_old + (1.0 - beta_one) * clipped
    second_new = beta_two * second_old + (1.0 - beta_two) * clipped * clipped
    bias_one = 1.0 - beta_one**STEP
    bias_two = 1.0 - beta_two**STEP
    direction = first_new / bias_one / (jnp.sqrt(second_new / bias_two) + 1e-08)
    blocks = clipped.reshape(clipped.shape[:-1] + (clipped.shape[-1] // QB, QB))
    first_bound = beta_one * first_scale + (1.0 - beta_one) * jnp.max(jnp.abs(blocks), axis=-1)
    second_bound = beta_two * second_scale + (1.0 - beta_two) * jnp.max(blocks * blocks, axis=-1)
    first_ratio = first_new / jnp.repeat(first_bound, QB, axis=-1)
    second_ratio = second_new / jnp.repeat(second_bound, QB, axis=-1)
    return (direction, first_ratio, second_ratio)


def project(left, right):
    return lax.dot_general(
        left, right, (((0,), (0,)), ((), ())), preferred_element_type=jnp.float32
    )


def on_device(
    section_inputs,
    top_grad,
    norm_gain,
    key_grad,
    value_grad,
    key_weight,
    value_weight,
    first_codes,
    second_codes,
    first_scale,
    second_scale,
):
    micro_count = top_grad.shape[0]
    token_count = top_grad.shape[1]
    width_local = top_grad.shape[2]
    row_count = micro_count * token_count
    section_count = lax.axis_size("section")
    is_last = lax.axis_index("section") == section_count - 1
    inputs = section_inputs[0].reshape(row_count, width_local)
    inputs_f = inputs.astype(jnp.float32)
    gain = norm_gain[0]
    keys_rows = key_grad[0].reshape(row_count, key_grad.shape[3])
    values_rows = value_grad[0].reshape(row_count, value_grad.shape[3])
    d_normed = jnp.dot(keys_rows, key_weight[0], preferred_element_type=jnp.float32) + jnp.dot(
        values_rows, value_weight[0], preferred_element_type=jnp.float32
    )
    local_power = jnp.sum(inputs_f * inputs_f, axis=1)
    local_dot = jnp.sum(inputs_f * gain * d_normed, axis=1)
    power, row_dot = lax.psum((local_power, local_dot), "shard")
    root = 1.0 / jnp.sqrt(power / D + 1e-05)
    normed = (inputs_f * root[:, None] * gain).astype(jnp.bfloat16)
    input_grad = (
        gain * d_normed * root[:, None] - inputs_f * (root * root * root * row_dot / D)[:, None]
    )
    top_rows = top_grad.reshape(row_count, width_local).astype(jnp.float32)
    base = input_grad + jnp.where(is_last, top_rows, jnp.zeros_like(top_rows))
    block_rows = row_count // section_count
    split_rows = base.reshape(section_count, block_rows, width_local)
    by_section = lax.all_to_all(split_rows, "section", split_axis=0, concat_axis=0, tiled=True)
    suffix = jnp.flip(jnp.cumsum(jnp.flip(by_section, 0), axis=0), 0).astype(jnp.bfloat16)
    returned = lax.all_to_all(suffix, "section", split_axis=0, concat_axis=0, tiled=True)
    leaving_rows = returned.reshape(row_count, width_local)
    leaving = leaving_rows.reshape(1, micro_count, token_count, width_local)
    gradients = jnp.stack([project(keys_rows, normed), project(values_rows, normed)])
    square_total = lax.psum(jnp.sum(gradients * gradients), ("section", "shard"))
    direction, first_ratio, second_ratio = optimizer(
        gradients, square_total, first_codes[0], second_codes[0], first_scale[0], second_scale[0]
    )
    return (direction[None], first_ratio[None], second_ratio[None], leaving)


def solution(mesh):
    return jax.shard_map(
        on_device,
        mesh=mesh,
        in_specs=(
            P("section", None, None, "shard"),
            P(None, None, "shard"),
            P("section", "shard"),
            P("section", None, None, None),
            P("section", None, None, None),
            P("section", None, "shard"),
            P("section", None, "shard"),
            P("section", None, None, "shard"),
            P("section", None, None, "shard"),
            P("section", None, None, "shard"),
            P("section", None, None, "shard"),
        ),
        out_specs=(
            P("section", None, None, "shard"),
            P("section", None, None, "shard"),
            P("section", None, None, "shard"),
            P("section", None, None, "shard"),
        ),
        check_vma=False,
    )
```

profile of v0, /device:TPU:0, one launch (start us, length us, event | category | flops | bytes accessed | tf_op | source)
XLA Modules:
  0.0 284.3 jit_solution(5729282218862681950)
XLA Ops:
  0.7 2.7 fusion.18
  3.5 5.6 %convert_select_fusion = f32[2,384,2048]{2,1,0:T(8,128)} fusion(bf16[2,384,2048]{2,1,0:T(8,128)(2,1)} %param.12, pred[]{:T(512)S(6)} %eq.5), kind=kLoop, calls=%fused_computation.46 | loop fusion | flops 3145728 | bytes 9437185 | tf_op jit(solution)/shard_map/jit(_where)/select_n | solution.py:81
  10.9 4.8 %fusion.22 = (f32[768]{0:T(1024)S(1)}, f32[768,2048]{1,0:T(8,128)}) fusion(bf16[1,2,384,2048]{3,2,1,0:T(8,128)(2,1)S(1)} %copy-done.6, f32[2048]{0:T(1024)S(1)} %bitcast.91, f32[768,2048]{1,0:T(8,128)S(1)} %fusion.30, bf16[768,512]{1,0:T(8,128)(2,1)S(1)} %bitcast.87, bf16[1,512,2048]{2,1,0:T(8,128)(2,1)S(1)} %copy-done), kind=kOutput, calls=%fused_computation.43 | convolution fusion | flops 1618476288 | bytes 18623488 | tf_op jit(solution)/shard_map/dot_general | solution.py:69
  15.8 18.3 %all-reduce = (f32[768]{0:T(1024)S(1)}, f32[768]{0:T(1024)S(1)}) all-reduce(f32[768]{0:T(1024)S(1)} %reduce_sum.30, f32[768]{0:T(1024)S(1)} %get-tuple-element.18), channel_id=1, replica_groups=mesh['section'=4,'shard'=8] {'shard'}, use_global_device_ids=true, to_apply=%region_1.0 | all-reduce | flops 1536 | bytes 12288 | tf_op jit(solution)/shard_map/psum | solution.py:74
  34.1 6.3 %bitcast_add_fusion = f32[768,2048]{1,0:T(8,128)S(1)} fusion(f32[2,384,2048]{2,1,0:T(8,128)} %convert_select_fusion, bf16[1,2,384,2048]{3,2,1,0:T(8,128)(2,1)} %param.11, f32[768,2048]{1,0:T(8,128)} %get-tuple-element.19, f32[768]{0:T(1024)S(1)} %get-tuple-element.16, f32[768]{0:T(1024)S(1)} %get-tuple-element.17, f32[2048]{0:T(1024)S(1)} %bitcast.92), kind=kLoop, calls=%fused_computation.34 | loop fusion | flops 9437184 | bytes 22034432 | tf_op jit(solution)/shard_map/add | solution.py:81
  40.4 71.3 %all_to_all.10 = f32[4,192,2048]{2,1,0:T(8,128)} all-to-all(f32[4,192,2048]{2,1,0:T(8,128)S(1)} %bitcast.86), channel_id=1, replica_groups=mesh['section'=4,'shard'=8] {'section'}, dimensions={0} | all-to-all | bytes 12582912 | tf_op jit(solution)/shard_map/all_to_all | solution.py:84
  111.8 6.3 %rev.7 = f32[4,192,2048]{2,1,0:T(8,128)} reverse(f32[4,192,2048]{2,1,0:T(8,128)} %all_to_all.10), dimensions={0} | reverse | bytes 12582912 | tf_op jit(solution)/shard_map/jit(_flip)/rev | solution.py:85
  118.1 4.8 %fusion.37 = bf16[4,192,2048]{2,1,0:T(8,128)(2,1)} fusion(f32[4,192,2048]{2,1,0:T(8,128)} %rev.7), kind=kOutput, calls=%fused_computation.62 | output fusion | flops 4718592 | bytes 9437184 | tf_op jit(solution)/shard_map/jit(cumsum)/reduce_window_sum | solution.py:85
  122.8 4.0 %rev.10 = bf16[4,192,2048]{2,1,0:T(8,128)(2,1)} reverse(bf16[4,192,2048]{2,1,0:T(8,128)(2,1)} %fusion.37), dimensions={0} | reverse | bytes 6291456 | tf_op jit(solution)/shard_map/jit(_flip)/rev | solution.py:85
  126.8 4.7 %all-to-all-start.1 = ((bf16[4,192,2048]{2,1,0:T(8,128)(2,1)}), bf16[4,192,2048]{2,1,0:T(8,128)(2,1)}, u32[]{:S(2)}, u32[]{:S(2)}) async-start(bf16[4,192,2048]{2,1,0:T(8,128)(2,1)} %rev.10), calls=%async_computation.1 | async-start | bytes 6291456 | tf_op jit(solution)/shard_map/all_to_all | solution.py:86
  131.5 4.1 %fusion.25 = f32[2048,512,1]{1,0,2:T(8,128)S(1)} fusion(bf16[1,2,384,2048]{3,2,1,0:T(8,128)(2,1)} %param.11, f32[2048]{0:T(1024)S(1)} %bitcast.93, f32[2,384]{1,0:T(2,128)S(1)} %mul.208, bf16[1,2,384,512]{3,2,1,0:T(8,128)(2,1)S(1)} %copy-done.8), kind=kOutput, calls=%fused_computation.49 | convolution fusion | flops 1616904192 | bytes 8137728 | tf_op jit(solution)/shard_map/dot_general | solution.py:40
  135.7 2.0 fusion.27
  137.7 1.9 copy-done.4
  139.7 2.8 fusion.12
  142.4 57.9 %psum.22 = f32[]{:T(128)} all-reduce(f32[]{:T(128)} %fusion.12), channel_id=1, replica_groups=mesh['section'=4,'shard'=8] {'section','shard'}, use_global_device_ids=true, to_apply=%region_3.0 | all-reduce | flops 1 | bytes 8 | tf_op jit(solution)/shard_map/psum | solution.py:90
  201.0 8.7 %copy.15 = s32[1,2,512,2048]{2,3,1,0:T(8,128)} copy(s32[1,2,512,2048]{3,2,1,0:T(8,128)} %param.18) | data formatting | bytes 16777216 | tf_op args[7]
  209.7 4.4 %multiply_reduce_fusion = (f32[2,512,16]{1,2,0:T(8,128)S(1)}, f32[2,512,16]{1,2,0:T(8,128)S(1)}) fusion(f32[1,512,16,128]{1,3,2,0:T(8,128)} %bitcast.79, f32[1,512,16,128]{1,3,2,0:T(8,128)} %bitcast.83, f32[]{:T(128)S(6)} %min.3), kind=kLoop, calls=%fused_computation.26 | loop fusion | flops 12550144 | bytes 8519684 | tf_op jit(solution)/shard_map/reduce_max | solution.py:33
  215.7 15.0 %bitcast_divide_fusion.1 = (f32[1,2,512,2048]{2,3,1,0:T(8,128)}, f32[1,2,512,2048]{2,3,1,0:T(8,128)}) fusion(f32[2,512,16]{1,2,0:T(8,128)S(1)} %get-tuple-element.21, f32[1,1,512,2048]{2,3,1,0:T(8,128)S(1)} %bitcast.81, f32[1,1,512,2048]{2,3,1,0:T(8,128)S(1)} %bitcast.85, f32[]{:T(128)S(6)} %min.3, s32[1,2,512,2048]{2,3,1,0:T(8,128)} %copy.15, ...), kind=kLoop, calls=%fused_computation.23 | loop fusion | flops 69206016 | bytes 33685508 | tf_op jit(solution)/shard_map/div | solution.py:34
  230.7 8.7 %copy.23 = f32[1,2,512,2048]{3,2,1,0:T(8,128)} copy(f32[1,2,512,2048]{2,3,1,0:T(8,128)} %get-tuple-element.12) | data formatting | bytes 16777216
  239.3 8.7 %copy.21 = s32[1,2,512,2048]{2,3,1,0:T(8,128)} copy(s32[1,2,512,2048]{3,2,1,0:T(8,128)} %param.19) | data formatting | bytes 16777216 | tf_op args[8]
  248.0 14.8 %bitcast_divide_fusion = (f32[1,2,512,2048]{2,3,1,0:T(8,128)}, f32[1,2,512,2048]{2,3,1,0:T(8,128)}) fusion(f32[2,512,16]{1,2,0:T(8,128)S(1)} %get-tuple-element.20, f32[1,1,512,2048]{2,3,1,0:T(8,128)} %bitcast.80, f32[1,1,512,2048]{2,3,1,0:T(8,128)} %bitcast.84, f32[]{:T(128)S(6)} %min.3, s32[1,2,512,2048]{2,3,1,0:T(8,128)} %copy.21, ...), kind=kLoop, calls=%fused_computation.22 | loop fusion | flops 31457280 | bytes 42074116 | tf_op jit(solution)/shard_map/div | solution.py:35
  262.8 8.7 %copy.24 = f32[1,2,512,2048]{3,2,1,0:T(8,128)} copy(f32[1,2,512,2048]{2,3,1,0:T(8,128)} %get-tuple-element.14) | data formatting | bytes 16777216
  271.5 8.8 %copy.22 = f32[1,2,512,2048]{3,2,1,0:T(8,128)} copy(f32[1,2,512,2048]{2,3,1,0:T(8,128)} %get-tuple-element.15) | data formatting | bytes 16777216
  280.3 4.0 %copy.28 = bf16[1,2,384,2048]{3,2,1,0:T(8,128)(2,1)} copy(bf16[1,2,384,2048]{3,2,1,0:T(8,128)(2,1)} %bitcast.29) | data formatting | bytes 6291456
  (35 shorter events, 3.5 us)
Async XLA Ops:
  0.6 10.3 %copy-start = (bf16[1,512,2048]{2,1,0:T(8,128)(2,1)S(1)}, bf16[1,512,2048]{2,1,0:T(8,128)(2,1)}, u32[]{:S(2)}) copy-start(bf16[1,512,2048]{2,1,0:T(8,128)(2,1)} %param.17) | copy-start | bytes 6291460
  3.4 5.7 %copy-start.9 = (bf16[1,512,2048]{2,1,0:T(8,128)(2,1)S(1)}, bf16[1,512,2048]{2,1,0:T(8,128)(2,1)}, u32[]{:S(2)}) copy-start(bf16[1,512,2048]{2,1,0:T(8,128)(2,1)} %param.16) | copy-start | bytes 6291460
  3.4 5.7 %copy-start.10 = (bf16[1,2,384,512]{3,2,1,0:T(8,128)(2,1)S(1)}, bf16[1,2,384,512]{3,2,1,0:T(8,128)(2,1)}, u32[]{:S(2)}) copy-start(bf16[1,2,384,512]{3,2,1,0:T(8,128)(2,1)} %param.14) | copy-start | bytes 2359300
  3.4 7.5 %copy-start.6 = (bf16[1,2,384,2048]{3,2,1,0:T(8,128)(2,1)S(1)}, bf16[1,2,384,2048]{3,2,1,0:T(8,128)(2,1)}, u32[]{:S(2)}) copy-start(bf16[1,2,384,2048]{3,2,1,0:T(8,128)(2,1)} %param.11) | copy-start | bytes 9437188
  3.4 7.5 %copy-start.8 = (bf16[1,2,384,512]{3,2,1,0:T(8,128)(2,1)S(1)}, bf16[1,2,384,512]{3,2,1,0:T(8,128)(2,1)}, u32[]{:S(2)}) copy-start(bf16[1,2,384,512]{3,2,1,0:T(8,128)(2,1)} %param.15) | copy-start | bytes 2359300
  3.4 7.5 %copy-start.14 = (f32[1,2048]{1,0:T(1,128)S(1)}, f32[1,2048]{1,0:T(1,128)}, u32[]{:S(2)}) copy-start(f32[1,2048]{1,0:T(1,128)} %param.13) | copy-start | bytes 24580
  126.8 153.5 %all-to-all-start.1 = ((bf16[4,192,2048]{2,1,0:T(8,128)(2,1)}), bf16[4,192,2048]{2,1,0:T(8,128)(2,1)}, u32[]{:S(2)}, u32[]{:S(2)}) async-start(bf16[4,192,2048]{2,1,0:T(8,128)(2,1)} %rev.10), calls=%async_computation.1 | async-start | bytes 6291456 | tf_op jit(solution)/shard_map/all_to_all | solution.py:86
  131.5 4.1 %copy-start.11 = (bf16[1,2,384,512]{3,2,1,0:T(8,128)(2,1)S(1)}, bf16[1,2,384,512]{3,2,1,0:T(8,128)(2,1)}, u32[]{:S(2)}) copy-start(bf16[1,2,384,512]{3,2,1,0:T(8,128)(2,1)} %param.14) | copy-start | bytes 2359300
  131.5 4.1 %copy-start.7 = (bf16[1,2,384,2048]{3,2,1,0:T(8,128)(2,1)S(1)}, bf16[1,2,384,2048]{3,2,1,0:T(8,128)(2,1)}, u32[]{:S(2)}) copy-start(bf16[1,2,384,2048]{3,2,1,0:T(8,128)(2,1)} %param.11) | copy-start | bytes 9437188
  135.6 2.1 copy-start.2
  137.7 2.0 copy-start.4
  209.7 4.4 %copy-start.12 = (f32[1,2,512,16]{2,3,1,0:T(8,128)S(1)}, f32[1,2,512,16]{2,3,1,0:T(8,128)}, u32[]{:S(2)}) copy-start(f32[1,2,512,16]{2,3,1,0:T(8,128)} %param.20) | copy-start | bytes 196612
  209.7 4.4 %copy-start.13 = (f32[1,2,512,16]{2,3,1,0:T(8,128)S(1)}, f32[1,2,512,16]{2,3,1,0:T(8,128)}, u32[]{:S(2)}) copy-start(f32[1,2,512,16]{2,3,1,0:T(8,128)} %param.21) | copy-start | bytes 196612
  209.7 4.7 %copy-start.3 = (f32[2048,512,1]{1,0,2:T(8,128)S(1)}, f32[2048,512,1]{1,0,2:T(8,128)}, u32[]{:S(2)}) copy-start(f32[2048,512,1]{1,0,2:T(8,128)} %copy-done.2) | copy-start | bytes 12582916
  209.7 6.0 %copy-start.5 = (f32[2048,512,1]{1,0,2:T(8,128)S(1)}, f32[2048,512,1]{1,0,2:T(8,128)}, u32[]{:S(2)}) copy-start(f32[2048,512,1]{1,0,2:T(8,128)} %copy-done.4) | copy-start | bytes 12582916
  271.5 12.8 %copy-start.1 = (bf16[1,512,2048]{2,1,0:T(8,128)(2,1)S(1)}, bf16[1,512,2048]{2,1,0:T(8,128)(2,1)}, u32[]{:S(2)}) copy-start(bf16[1,512,2048]{2,1,0:T(8,128)(2,1)} %param.17) | copy-start | bytes 6291460
where the time goes:
time: 285 us; the launch traced here: 284 us
  blocking collectives  147 us (52%)
  local copies, waits for them, and re-layouts  61.3 us (22%)
  other arithmetic  56.4 us (20%)
  matrix products  12.8 us (4%)
  starting transfers between devices  4.66 us (2%)
    all_to_all x1, blocking collectives, on_device(): lax.all_to_all(split_rows, 'section', split_axis=0, concat_axis=0, tiled=...  71.3 us
    psum x1, blocking collectives, on_device(): lax.psum(jnp.sum(gradients * gradients), ('section', 'shard'))  57.9 us
    unnamed x36, local copies, waits for them, and re-layouts  51 us
    psum x1, blocking collectives, on_device(): power, row_dot = lax.psum((local_power, local_dot), 'shard')  18.3 us
    div x1, other arithmetic, optimizer(): first_ratio = first_new / jnp.repeat(first_bound, QB, axis=-1)  15 us
    div x1, other arithmetic, optimizer(): second_ratio = second_new / jnp.repeat(second_bound, QB, axis=-1)  14.8 us
    add x1, other arithmetic, on_device(): base = input_grad + jnp.where(is_last, top_rows, jnp.zeros_like(top_rows))  6.35 us
    rev x1, local copies, waits for them, and re-layouts, on_device(): jnp.flip(by_section, 0)  6.28 us
  transfers between devices with their start and end apart: 1, of which 0 were waited for; matrix products, arithmetic and copies ran while one was open for 30% of the time, Pallas kernels for 0%

commit v1 on v0

v1 whole, which is shorter than its diff:
```python
import functools

import jax
import jax.numpy as jnp
from jax import lax
from jax.experimental import pallas as pl
from jax.experimental.pallas import tpu as pltpu
from jax.sharding import PartitionSpec as P

D = 16384
QB = 128
STEP = 20

beta_one = 0.9
beta_two = 0.95
clip_norm = 1.0
MIB = 1 << 20


def optimizer_body(
    total_ref, grad_ref, first_ref, second_ref, fscale_ref, sscale_ref, dir_ref, fr_ref, sr_ref
):
    clip_factor = jnp.minimum(1.0, clip_norm / (jnp.sqrt(total_ref[0:1, 0:1]) + 1e-06))
    inv_one = 1.0 / (1.0 - beta_one**STEP)
    inv_two = 1.0 / (1.0 - beta_two**STEP)
    fscale = fscale_ref[0]
    sscale = sscale_ref[0]
    for block in range(grad_ref.shape[2] // QB):
        cols = slice(block * QB, (block + 1) * QB)
        grad = clip_factor * grad_ref[0, :, cols]
        peak = jnp.max(jnp.abs(grad), axis=1, keepdims=True)
        f_scale = fscale[:, block : block + 1]
        s_scale = sscale[:, block : block + 1]
        f_code = first_ref[0, :, cols]
        s_code = second_ref[0, :, cols]
        f_power = lax.shift_right_logical(jnp.full_like(f_code, 128), f_code & 7)
        f_power = jnp.where(f_code >= 8, -f_power, f_power).astype(jnp.float32)
        s_power = lax.shift_right_logical(jnp.full_like(s_code, 32768), s_code).astype(jnp.float32)
        first_new = (f_scale * (beta_one / 128.0)) * f_power + (1.0 - beta_one) * grad
        second_new = (s_scale * (beta_two / 32768.0)) * s_power + (1.0 - beta_two) * grad * grad
        f_bound = 1.0 / (beta_one * f_scale + (1.0 - beta_one) * peak)
        s_bound = 1.0 / (beta_two * s_scale + (1.0 - beta_two) * peak * peak)
        dir_ref[0, :, cols] = first_new * inv_one / (jnp.sqrt(second_new * inv_two) + 1e-08)
        fr_ref[0, :, cols] = first_new * f_bound
        sr_ref[0, :, cols] = second_new * s_bound


def optimizer(total, gradients, first_codes, second_codes, first_scale, second_scale):
    stacks, features, width = gradients.shape
    rows = features // 4
    while rows > 128 and rows % 2 == 0:
        rows //= 2
    scales = width // QB

    def spec(columns):
        return pl.BlockSpec((1, rows, columns), lambda i, j: (i, j, 0))

    out = jax.ShapeDtypeStruct(gradients.shape, jnp.float32)
    count = stacks * features * width
    return pl.pallas_call(
        optimizer_body,
        grid=(stacks, features // rows),
        in_specs=[pl.BlockSpec((8, 128), lambda i, j: (0, 0))]
        + [spec(width)] * 3
        + [spec(scales)] * 2,
        out_specs=[spec(width)] * 3,
        out_shape=[out] * 3,
        compiler_params=pltpu.CompilerParams(vmem_limit_bytes=40 * MIB),
        cost_estimate=pl.CostEstimate(
            flops=40 * count, bytes_accessed=24 * count, transcendentals=2 * count
        ),
    )(total, gradients, first_codes, second_codes, first_scale, second_scale)


def project(left, right):
    return lax.dot_general(
        left, right, (((0,), (0,)), ((), ())), preferred_element_type=jnp.float32
    )


def on_device(
    section_inputs,
    top_grad,
    norm_gain,
    key_grad,
    value_grad,
    key_weight,
    value_weight,
    first_codes,
    second_codes,
    first_scale,
    second_scale,
):
    micro_count, token_count, width_local = top_grad.shape
    row_count = micro_count * token_count
    section_count = lax.axis_size("section")
    inputs = section_inputs[0].reshape(row_count, width_local)
    inputs_f = inputs.astype(jnp.float32)
    gain = norm_gain[0]
    keys_rows = key_grad[0].reshape(row_count, key_grad.shape[3])
    values_rows = value_grad[0].reshape(row_count, value_grad.shape[3])
    d_normed = jnp.dot(keys_rows, key_weight[0], preferred_element_type=jnp.float32) + jnp.dot(
        values_rows, value_weight[0], preferred_element_type=jnp.float32
    )
    local_power = jnp.sum(inputs_f * inputs_f, axis=1)
    local_dot = jnp.sum(inputs_f * gain * d_normed, axis=1)
    power, row_dot = lax.psum((local_power, local_dot), "shard")
    root = 1.0 / jnp.sqrt(power / D + 1e-05)
    normed = (inputs_f * root[:, None] * gain).astype(jnp.bfloat16)
    input_grad = (
        gain * d_normed * root[:, None] - inputs_f * (root * root * root * row_dot / D)[:, None]
    ).astype(jnp.bfloat16)
    block_rows = row_count // section_count
    gradients = jnp.stack([project(keys_rows, normed), project(values_rows, normed)])
    square_total = lax.psum(jnp.sum(gradients * gradients), ("section", "shard"))
    split_rows = input_grad.reshape(section_count, block_rows, width_local)
    by_section = lax.all_to_all(split_rows, "section", split_axis=0, concat_axis=0, tiled=True)
    top_rows = top_grad.reshape(section_count, block_rows, width_local)
    running = lax.dynamic_index_in_dim(
        top_rows, lax.axis_index("section"), 0, keepdims=False
    ).astype(jnp.float32)
    suffix = [None] * section_count
    for section in range(section_count - 1, -1, -1):
        running = running + by_section[section].astype(jnp.float32)
        suffix[section] = running.astype(jnp.bfloat16)
    returned = lax.all_to_all(
        jnp.stack(suffix), "section", split_axis=0, concat_axis=0, tiled=True
    )
    leaving = returned.reshape(1, micro_count, token_count, width_local)
    direction, first_ratio, second_ratio = optimizer(
        jnp.broadcast_to(square_total, (8, 128)),
        gradients,
        first_codes[0],
        second_codes[0],
        first_scale[0],
        second_scale[0],
    )
    return (direction[None], first_ratio[None], second_ratio[None], leaving)


def solution(mesh):
    sharded = P("section", None, None, "shard")
    whole_rows = P("section", None, None, None)
    return jax.shard_map(
        on_device,
        mesh=mesh,
        in_specs=(
            sharded,
            P(None, None, "shard"),
            P("section", "shard"),
            whole_rows,
            whole_rows,
            P("section", None, "shard"),
            P("section", None, "shard"),
            sharded,
            sharded,
            sharded,
            sharded,
        ),
        out_specs=(sharded, sharded, sharded, sharded),
        check_vma=False,
    )
```

time: 285 us -> 185 us (0.65)
  blocking collectives: 147 us -> 76 us
  local copies, waits for them, and re-layouts: 61.3 us -> 8.46 us
  other arithmetic: 56.4 us -> 18.2 us
  waiting for transfers between devices: 0.01 us -> 33.6 us
  Pallas kernels: 0 us -> 23.3 us
  starting transfers between devices: 4.66 us -> 9.31 us
    all_to_all x1 -> x0, blocking collectives: 71.3 us -> none  [on_device(): lax.all_to_all(split_rows, 'section', split_axis=0, concat_axis=0, tiled=...]
    unnamed x36 -> x23, local copies, waits for them, and re-layouts: 51 us -> 7.79 us
    all_to_all x1 -> x2, waiting for transfers between devices: 0.01 us -> 33.6 us  [the longest x1 33.6 us: on_device(): lax.all_to_all(split_rows, 'section', split_axis=0, concat_axis=0, tiled=...]
    div x2 -> x0, other arithmetic: 29.8 us -> none  [the longest x1 15 us: optimizer(): first_ratio = first_new / jnp.repeat(first_bound, QB, axis=-1)]
    pallas_call x0 -> x1, Pallas kernels: none -> 23.3 us  [optimizer(): pl.pallas_call(optimizer_body, grid=(stacks, features // rows), in_specs=...]
    rev x2 -> x0, local copies, waits for them, and re-layouts: 10.3 us -> none  [the longest x1 6.28 us: on_device(): jnp.flip(by_section, 0)]
    convert_element_type x0 -> x2, other arithmetic: none -> 8.52 us  [the longest x1 5.58 us: on_device(): input_grad = (gain * d_normed * root[:, None] - inputs_f * (root * root *...]
    add x2 -> x0, other arithmetic: 6.37 us -> none  [the longest x1 6.35 us: on_device(): base = input_grad + jnp.where(is_last, top_rows, jnp.zeros_like(top_rows))]
  transfers between devices with their start and end apart: 1 -> 2, of which waited for: 0 -> 1; matrix products, arithmetic and copies ran while one was open for 30% -> 7% of each run, Pallas kernels for 0% -> 13%
where the time goes in v1:
time: 185 us
  blocking collectives  76 us (41%)
  waiting for transfers between devices  33.6 us (18%)
  Pallas kernels  23.3 us (13%)
  other arithmetic  18.2 us (10%)
  matrix products  14.7 us (8%)
  starting transfers between devices  9.31 us (5%)
  local copies, waits for them, and re-layouts  8.46 us (5%)
    psum x1, blocking collectives, on_device(): lax.psum(jnp.sum(gradients * gradients), ('section', 'shard'))  57.7 us
    all_to_all x1, waiting for transfers between devices, on_device(): lax.all_to_all(split_rows, 'section', split_axis=0, concat_axis=0, tiled=...  33.6 us
    pallas_call x1, Pallas kernels, optimizer(): pl.pallas_call(optimizer_body, grid=(stacks, features // rows), in_specs=...  23.3 us
    psum x1, blocking collectives, on_device(): power, row_dot = lax.psum((local_power, local_dot), 'shard')  18.3 us
    unnamed x23, local copies, waits for them, and re-layouts  7.79 us
    dot_general x2, matrix products, project(): lax.dot_general(left, right, (((0,), (0,)), ((), ())), preferred_element_...  6.09 us
    convert_element_type x1, other arithmetic, on_device(): input_grad = (gain * d_normed * root[:, None] - inputs_f * (root * root *...  5.58 us
    another operation x1, other arithmetic, on_device(): jnp.stack([project(keys_rows, normed), project(values_rows, normed)])  5.09 us
  transfers between devices with their start and end apart: 2, of which 1 were waited for; matrix products, arithmetic and copies ran while one was open for 7% of the time, Pallas kernels for 13%

profile of v1, /device:TPU:0, one launch (start us, length us, event | category | flops | bytes accessed | tf_op | source)
XLA Modules:
  0.0 184.5 jit_solution(1393622676715045162)
XLA Ops:
  0.6 0.0 copy-start
  0.6 2.7 %fusion = f32[2,384]{1,0:T(2,128)S(1)} fusion(bf16[1,2,384,2048]{3,2,1,0:T(8,128)(2,1)} %param.11), kind=kLoop, calls=%fused_computation.6 | loop fusion | flops 4717824 | bytes 3148800 | tf_op jit(solution)/shard_map/reduce_sum | solution.py:105
  3.4 0.0 copy-start.5
  3.4 0.0 copy-start.7
  3.4 3.8 %fusion.11 = f32[768,2048]{1,0:T(8,128)S(1)} fusion(bf16[768,512]{1,0:T(8,128)(2,1)} %bitcast.62, bf16[1,512,2048]{2,1,0:T(8,128)(2,1)} %param.16), kind=kOutput, calls=%fused_computation.19 | convolution fusion | flops 1610612736 | bytes 9175040 | tf_op jit(solution)/shard_map/dot_general | solution.py:102
  7.2 4.9 %fusion.4 = (f32[768]{0:T(1024)S(1)}, f32[768,2048]{1,0:T(8,128)}) fusion(bf16[1,2,384,2048]{3,2,1,0:T(8,128)(2,1)S(1)} %copy-done.3, f32[2048]{0:T(1024)S(1)} %bitcast.64, f32[768,2048]{1,0:T(8,128)S(1)} %fusion.11, bf16[768,512]{1,0:T(8,128)(2,1)S(1)} %bitcast.61, bf16[1,512,2048]{2,1,0:T(8,128)(2,1)S(1)} %copy-done), kind=kOutput, calls=%fused_computation.10 | convolution fusion | flops 1618476288 | bytes 18623488 | tf_op jit(solution)/shard_map/dot_general | solution.py:102
  12.1 18.3 %all-reduce = (f32[768]{0:T(1024)S(1)}, f32[768]{0:T(1024)S(1)}) all-reduce(f32[768]{0:T(1024)S(1)} %reduce_sum.30, f32[768]{0:T(1024)S(1)} %get-tuple-element.20), channel_id=1, replica_groups=mesh['section'=4,'shard'=8] {'shard'}, use_global_device_ids=true, to_apply=%region_1.0 | all-reduce | flops 1536 | bytes 12288 | tf_op jit(solution)/shard_map/psum | solution.py:107
  30.4 5.6 %fusion.6 = bf16[768,2048]{1,0:T(8,128)(2,1)} fusion(bf16[1,2,384,2048]{3,2,1,0:T(8,128)(2,1)} %param.11, f32[768,2048]{1,0:T(8,128)} %get-tuple-element.21, f32[768]{0:T(1024)S(1)} %get-tuple-element.18, f32[768]{0:T(1024)S(1)} %get-tuple-element.19, f32[2048]{0:T(1024)S(1)} %bitcast.65), kind=kLoop, calls=%fused_computation.12 | loop fusion | flops 9437184 | bytes 12597248 | tf_op jit(solution)/shard_map/convert_element_type | solution.py:112
  36.0 4.7 %all-to-all-start = ((bf16[4,192,2048]{2,1,0:T(8,128)(2,1)}), bf16[4,192,2048]{2,1,0:T(8,128)(2,1)}, u32[]{:S(2)}, u32[]{:S(2)}) async-start(bf16[4,192,2048]{2,1,0:T(8,128)(2,1)} %bitcast.58), calls=%async_computation | async-start | bytes 6291456 | tf_op jit(solution)/shard_map/all_to_all | solution.py:117
  40.7 33.6 %all-to-all-done = bf16[4,192,2048]{2,1,0:T(8,128)(2,1)} async-done(((bf16[4,192,2048]{2,1,0:T(8,128)(2,1)}), bf16[4,192,2048]{2,1,0:T(8,128)(2,1)}, u32[]{:S(2)}, u32[]{:S(2)}) %all-to-all-start) | async-done | bytes 3145760 | tf_op jit(solution)/shard_map/all_to_all | solution.py:117
  74.2 2.9 %add_convert_fusion = (bf16[1,192,2048]{2,1,0:T(8,128)(2,1)S(1)}, bf16[1,192,2048]{2,1,0:T(8,128)(2,1)S(1)}, bf16[1,192,2048]{2,1,0:T(8,128)(2,1)S(1)}, bf16[1,192,2048]{2,1,0:T(8,128)(2,1)S(1)}) fusion(bf16[4,192,2048]{2,1,0:T(8,128)(2,1)} %all-to-all-done, bf16[4,192,2048]{2,1,0:T(8,128)(2,1)} %bitcast.63, s32[]{:T(128)S(6)} %select_n.4), kind=kLoop, calls=%fused_computation.21 | loop fusion | flops 5111808 | bytes 7077892 | tf_op jit(solution)/shard_map/convert_element_type | solution.py:125
  77.2 1.9 %pad_maximum_fusion.1 = bf16[4,192,2048]{2,1,0:T(8,128)(2,1)} fusion(bf16[1,192,2048]{2,1,0:T(8,128)(2,1)S(1)} %get-tuple-element.17, bf16[1,192,2048]{2,1,0:T(8,128)(2,1)S(1)} %get-tuple-element.16, bf16[1,192,2048]{2,1,0:T(8,128)(2,1)S(1)} %get-tuple-element.15, bf16[1,192,2048]{2,1,0:T(8,128)(2,1)S(1)} %get-tuple-element.14), kind=kLoop, calls=%fused_computation.17 | loop fusion | flops 4718592 | bytes 6291456 | tf_op jit(solution)/shard_map/stack | solution.py:127
  79.1 4.7 %all-to-all-start.1 = ((bf16[4,192,2048]{2,1,0:T(8,128)(2,1)}), bf16[4,192,2048]{2,1,0:T(8,128)(2,1)}, u32[]{:S(2)}, u32[]{:S(2)}) async-start(bf16[4,192,2048]{2,1,0:T(8,128)(2,1)} %pad_maximum_fusion.1), calls=%async_computation.1 | async-start | bytes 6291456 | tf_op jit(solution)/shard_map/all_to_all | solution.py:126
  83.8 0.0 copy-start.6
  83.8 4.0 %convolution_bitcast_fusion = f32[1,512,2048]{2,1,0:T(8,128)S(1)} fusion(bf16[1,2,384,2048]{3,2,1,0:T(8,128)(2,1)} %param.11, f32[2048]{0:T(1024)S(1)} %bitcast.66, f32[2,384]{1,0:T(2,128)S(1)} %mul.74, bf16[1,2,384,512]{3,2,1,0:T(8,128)(2,1)S(1)} %copy-done.5), kind=kOutput, calls=%fused_computation.14 | convolution fusion | flops 1616904192 | bytes 8137728 | tf_op jit(solution)/shard_map/dot_general | solution.py:76
  87.8 2.1 %convolution_bitcast_fusion.1 = f32[1,512,2048]{2,1,0:T(8,128)S(1)} fusion(bf16[1,2,384,2048]{3,2,1,0:T(8,128)(2,1)S(1)} %copy-done.4, f32[2048]{0:T(1024)S(1)} %bitcast.67, f32[2,384]{1,0:T(2,128)S(1)} %mul.74, bf16[1,2,384,512]{3,2,1,0:T(8,128)(2,1)S(1)} %copy-done.6), kind=kOutput, calls=%fused_computation.15 | convolution fusion | flops 1616904192 | bytes 8137728 | tf_op jit(solution)/shard_map/dot_general | solution.py:76
  89.9 5.1 %pad_maximum_fusion = (f32[2,512,2048]{2,1,0:T(8,128)}, f32[]{:T(128)}) fusion(f32[1,512,2048]{2,1,0:T(8,128)S(1)} %convolution_bitcast_fusion, f32[1,512,2048]{2,1,0:T(8,128)S(1)} %convolution_bitcast_fusion.1), kind=kLoop, calls=%fused_computation | loop fusion | flops 6291455 | bytes 16777220 | tf_op jit(solution)/shard_map/stack | solution.py:114
  95.0 57.7 %psum.22 = f32[]{:T(128)} all-reduce(f32[]{:T(128)} %get-tuple-element.13), channel_id=1, replica_groups=mesh['section'=4,'shard'=8] {'section','shard'}, use_global_device_ids=true, to_apply=%region_3.0 | all-reduce | flops 1 | bytes 8 | tf_op jit(solution)/shard_map/psum | solution.py:115
  152.8 0.2 copy.19
  153.0 0.2 copy.20
  153.2 0.7 broadcast_in_dim.15.total_ref
  153.8 3.4 %copy-done.2 = f32[2,512,2048]{2,1,0:T(8,128)S(1)} copy-done((f32[2,512,2048]{2,1,0:T(8,128)S(1)}, f32[2,512,2048]{2,1,0:T(8,128)}, u32[]{:S(2)}) %copy-start.2) | copy-done | bytes 8388632
  157.2 23.3 %shard_map.138 = (f32[2,512,2048]{2,1,0:T(8,128)}, f32[2,512,2048]{2,1,0:T(8,128)}, f32[2,512,2048]{2,1,0:T(8,128)}) custom-call(f32[8,128]{1,0:T(8,128)S(1)} %broadcast_in_dim.15.total_ref, f32[2,512,2048]{2,1,0:T(8,128)S(1)} %copy-done.2, s32[2,512,2048]{2,1,0:T(8,128)} %bitcast.59, s32[2,512,2048]{2,1,0:T(8,128)} %bitcast.60, f32[2,512,16]{2,1,0:T(8,128)S(1)} %bitcast.56, ...), custom_call_target="tpu_custom_call" | custom-call | flops 83886080 | bytes 50331648 | tf_op jit(solution)/shard_map/pallas_call | solution.py:60
  180.6 4.0 %copy.28 = bf16[1,2,384,2048]{3,2,1,0:T(8,128)(2,1)} copy(bf16[1,2,384,2048]{3,2,1,0:T(8,128)(2,1)} %bitcast.24) | data formatting | bytes 6291456
  (19 shorter events, 0.1 us)
Async XLA Ops:
  0.6 6.6 %copy-start = (bf16[1,512,2048]{2,1,0:T(8,128)(2,1)S(1)}, bf16[1,512,2048]{2,1,0:T(8,128)(2,1)}, u32[]{:S(2)}) copy-start(bf16[1,512,2048]{2,1,0:T(8,128)(2,1)} %param.17) | copy-start | bytes 6291460
  3.4 3.8 %copy-start.3 = (bf16[1,2,384,2048]{3,2,1,0:T(8,128)(2,1)S(1)}, bf16[1,2,384,2048]{3,2,1,0:T(8,128)(2,1)}, u32[]{:S(2)}) copy-start(bf16[1,2,384,2048]{3,2,1,0:T(8,128)(2,1)} %param.11) | copy-start | bytes 9437188
  3.4 3.8 %copy-start.5 = (bf16[1,2,384,512]{3,2,1,0:T(8,128)(2,1)S(1)}, bf16[1,2,384,512]{3,2,1,0:T(8,128)(2,1)}, u32[]{:S(2)}) copy-start(bf16[1,2,384,512]{3,2,1,0:T(8,128)(2,1)} %param.15) | copy-start | bytes 2359300
  3.4 3.8 %copy-start.7 = (f32[1,2048]{1,0:T(1,128)S(1)}, f32[1,2048]{1,0:T(1,128)}, u32[]{:S(2)}) copy-start(f32[1,2048]{1,0:T(1,128)} %param.13) | copy-start | bytes 24580
  36.0 38.2 %all-to-all-start = ((bf16[4,192,2048]{2,1,0:T(8,128)(2,1)}), bf16[4,192,2048]{2,1,0:T(8,128)(2,1)}, u32[]{:S(2)}, u32[]{:S(2)}) async-start(bf16[4,192,2048]{2,1,0:T(8,128)(2,1)} %bitcast.58), calls=%async_computation | async-start | bytes 6291456 | tf_op jit(solution)/shard_map/all_to_all | solution.py:117
  79.1 101.5 %all-to-all-start.1 = ((bf16[4,192,2048]{2,1,0:T(8,128)(2,1)}), bf16[4,192,2048]{2,1,0:T(8,128)(2,1)}, u32[]{:S(2)}, u32[]{:S(2)}) async-start(bf16[4,192,2048]{2,1,0:T(8,128)(2,1)} %pad_maximum_fusion.1), calls=%async_computation.1 | async-start | bytes 6291456 | tf_op jit(solution)/shard_map/all_to_all | solution.py:126
  83.7 4.1 %copy-start.4 = (bf16[1,2,384,2048]{3,2,1,0:T(8,128)(2,1)S(1)}, bf16[1,2,384,2048]{3,2,1,0:T(8,128)(2,1)}, u32[]{:S(2)}) copy-start(bf16[1,2,384,2048]{3,2,1,0:T(8,128)(2,1)} %param.11) | copy-start | bytes 9437188
  83.8 4.1 %copy-start.6 = (bf16[1,2,384,512]{3,2,1,0:T(8,128)(2,1)S(1)}, bf16[1,2,384,512]{3,2,1,0:T(8,128)(2,1)}, u32[]{:S(2)}) copy-start(bf16[1,2,384,512]{3,2,1,0:T(8,128)(2,1)} %param.14) | copy-start | bytes 2359300
  89.9 62.9 %copy-start.8 = (f32[1,2,512,16]{2,3,1,0:T(8,128)S(1)}, f32[1,2,512,16]{2,3,1,0:T(8,128)}, u32[]{:S(2)}) copy-start(f32[1,2,512,16]{2,3,1,0:T(8,128)} %param.20) | copy-start | bytes 196612
  89.9 63.1 %copy-start.9 = (f32[1,2,512,16]{2,3,1,0:T(8,128)S(1)}, f32[1,2,512,16]{2,3,1,0:T(8,128)}, u32[]{:S(2)}) copy-start(f32[1,2,512,16]{2,3,1,0:T(8,128)} %param.21) | copy-start | bytes 196612
  153.8 3.4 %copy-start.2 = (f32[2,512,2048]{2,1,0:T(8,128)S(1)}, f32[2,512,2048]{2,1,0:T(8,128)}, u32[]{:S(2)}) copy-start(f32[2,512,2048]{2,1,0:T(8,128)} %get-tuple-element.12.grad_ref) | copy-start | bytes 25165828
  157.2 27.3 %copy-start.1 = (bf16[1,512,2048]{2,1,0:T(8,128)(2,1)S(1)}, bf16[1,512,2048]{2,1,0:T(8,128)(2,1)}, u32[]{:S(2)}) copy-start(bf16[1,512,2048]{2,1,0:T(8,128)(2,1)} %param.17) | copy-start | bytes 6291460

commit v2 on v1

--- a/solution.py
+++ b/solution.py
@@ -72,6 +72,68 @@
     )(total, gradients, first_codes, second_codes, first_scale, second_scale)
 
 
+def reduce_body(axes, x_ref, out_ref, *scratch):
+    barrier = pltpu.get_barrier_semaphore()
+    peers = 0
+    for axis, size in axes:
+        me = lax.axis_index(axis)
+        for step in range(1, size):
+            pl.semaphore_signal(
+                barrier,
+                inc=1,
+                device_id={axis: lax.rem(me + step, size)},
+                device_id_type=pl.DeviceIdType.MESH,
+            )
+            peers += 1
+    pl.semaphore_wait(barrier, peers)
+    value = x_ref[...]
+    for at, (axis, size) in enumerate(axes):
+        slots, send, receive = scratch[3 * at : 3 * at + 3]
+        me = lax.axis_index(axis)
+        slots[0] = value
+        copies = []
+        for step in range(1, size):
+            copy = pltpu.make_async_remote_copy(
+                src_ref=slots.at[0],
+                dst_ref=slots.at[step],
+                send_sem=send.at[step],
+                recv_sem=receive.at[step],
+                device_id={axis: lax.rem(me + step, size)},
+                device_id_type=pl.DeviceIdType.MESH,
+            )
+            copy.start()
+            copies.append(copy)
+        for copy in copies:
+            copy.wait()
+        value = slots[0]
+        for step in range(1, size):
+            value = value + slots[step]
+    out_ref[...] = value
+
+
+def reduce_over(x, axis_names, identity):
+    axes = [(axis, lax.axis_size(axis)) for axis in axis_names]
+    if max(size for _, size in axes) > 8:
+        return lax.psum(x, axis_names)
+    scratch = []
+    for _, size in axes:
+        scratch += [
+            pltpu.VMEM((size,) + x.shape, jnp.float32),
+            pltpu.SemaphoreType.DMA((size,)),
+            pltpu.SemaphoreType.DMA((size,)),
+        ]
+    vmem = pl.BlockSpec(memory_space=pltpu.VMEM)
+    return pl.pallas_call(
+        functools.partial(reduce_body, axes),
+        in_specs=[vmem],
+        out_specs=vmem,
+        out_shape=jax.ShapeDtypeStruct(x.shape, jnp.float32),
+        scratch_shapes=scratch,
+        compiler_params=pltpu.CompilerParams(collective_id=identity, has_side_effects=True),
+        cost_estimate=pl.CostEstimate(flops=10000, bytes_accessed=1 << 20, transcendentals=0),
+    )(x)
+
+
 def project(left, right):
     return lax.dot_general(
         left, right, (((0,), (0,)), ((), ())), preferred_element_type=jnp.float32
@@ -104,7 +166,10 @@
     )
     local_power = jnp.sum(inputs_f * inputs_f, axis=1)
     local_dot = jnp.sum(inputs_f * gain * d_normed, axis=1)
-    power, row_dot = lax.psum((local_power, local_dot), "shard")
+    lanes = jnp.stack([local_power, local_dot]).reshape(-1, 128)
+    lane_rows = lanes.shape[0]
+    lanes = jnp.pad(lanes, ((0, -lane_rows % 8), (0, 0)))
+    power, row_dot = reduce_over(lanes, ("shard",), 0)[:lane_rows].reshape(2, row_count)
     root = 1.0 / jnp.sqrt(power / D + 1e-05)
     normed = (inputs_f * root[:, None] * gain).astype(jnp.bfloat16)
     input_grad = (
@@ -112,9 +177,11 @@
     ).astype(jnp.bfloat16)
     block_rows = row_count // section_count
     gradients = jnp.stack([project(keys_rows, normed), project(values_rows, normed)])
-    square_total = lax.psum(jnp.sum(gradients * gradients), ("section", "shard"))
     split_rows = input_grad.reshape(section_count, block_rows, width_local)
     by_section = lax.all_to_all(split_rows, "section", split_axis=0, concat_axis=0, tiled=True)
+    partial = jnp.broadcast_to(jnp.sum(gradients * gradients), (8, 128))
+    square_total = reduce_over(partial, ("shard", "section"), 1)
+    by_section, square_total = lax.optimization_barrier((by_section, square_total))
     top_rows = top_grad.reshape(section_count, block_rows, width_local)
     running = lax.dynamic_index_in_dim(
         top_rows, lax.axis_index("section"), 0, keepdims=False
@@ -123,12 +190,13 @@
     for section in range(section_count - 1, -1, -1):
         running = running + by_section[section].astype(jnp.float32)
         suffix[section] = running.astype(jnp.bfloat16)
+    suffix, square_total = lax.optimization_barrier((jnp.stack(suffix), square_total))
     returned = lax.all_to_all(
-        jnp.stack(suffix), "section", split_axis=0, concat_axis=0, tiled=True
+        suffix, "section", split_axis=0, concat_axis=0, tiled=True
     )
     leaving = returned.reshape(1, micro_count, token_count, width_local)
     direction, first_ratio, second_ratio = optimizer(
-        jnp.broadcast_to(square_total, (8, 128)),
+        square_total,
         gradients,
         first_codes[0],
         second_codes[0],

time: 185 us -> 122 us (0.66)
  blocking collectives: 76 us -> 0 us
  Pallas kernels: 23.3 us -> 58.3 us
  waiting for transfers between devices: 33.6 us -> 8.25 us
    psum x2 -> x0, blocking collectives: 76 us -> none  [the longest x1 57.7 us: on_device(): lax.psum(jnp.sum(gradients * gradients), ('section', 'shard'))]
    pallas_call x0 -> x2, Pallas kernels: none -> 35 us  [reduce_over(): pl.pallas_call(functools.partial(reduce_body, axes), in_specs=[vmem], out...]
    all_to_all x1, waiting for transfers between devices: 33.6 us -> 0.01 us  [on_device(): lax.all_to_all(split_rows, 'section', split_axis=0, concat_axis=0, tiled=...]
    all_to_all x1, waiting for transfers between devices: 0.01 us -> 8.25 us  [on_device(): lax.all_to_all(suffix, 'section', split_axis=0, concat_axis=0, tiled=True)]
    unnamed x23 -> x26, local copies, waits for them, and re-layouts: 7.79 us -> 7.8 us
  transfers between devices with their start and end apart: 2 -> 2, of which waited for: 1 -> 1; matrix products, arithmetic and copies ran while one was open for 7% -> 11% of each run, Pallas kernels for 13% -> 41%
where the time goes in v2:
time: 122 us; the launch traced here: 121 us
  Pallas kernels  58.3 us (48%)
  other arithmetic  19.7 us (16%)
  matrix products  14.7 us (12%)
  local copies, waits for them, and re-layouts  9.66 us (8%)
  starting transfers between devices  9.61 us (8%)
  waiting for transfers between devices  8.25 us (7%)
    pallas_call x2, Pallas kernels, reduce_over(): pl.pallas_call(functools.partial(reduce_body, axes), in_specs=[vmem], out...  35 us
    pallas_call x1, Pallas kernels, optimizer(): pl.pallas_call(optimizer_body, grid=(stacks, features // rows), in_specs=...  23.3 us
    all_to_all x1, waiting for transfers between devices, on_device(): lax.all_to_all(suffix, 'section', split_axis=0, concat_axis=0, tiled=True)  8.25 us
    unnamed x26, local copies, waits for them, and re-layouts  7.8 us
    dot_general x2, matrix products, project(): lax.dot_general(left, right, (((0,), (0,)), ((), ())), preferred_element_...  6.09 us
    convert_element_type x1, other arithmetic, on_device(): input_grad = (gain * d_normed * root[:, None] - inputs_f * (root * root *...  5.58 us
    another operation x1, other arithmetic, on_device(): jnp.stack([project(keys_rows, normed), project(values_rows, normed)])  5.09 us
    all_to_all x1, starting transfers between devices, on_device(): lax.all_to_all(suffix, 'section', split_axis=0, concat_axis=0, tiled=True)  4.96 us
  transfers between devices with their start and end apart: 2, of which 1 were waited for; matrix products, arithmetic and copies ran while one was open for 11% of the time, Pallas kernels for 41%

profile of v2, /device:TPU:0, one launch (start us, length us, event | category | flops | bytes accessed | tf_op | source)
XLA Modules:
  0.0 121.1 jit_solution(8536463362192530169)
XLA Ops:
  0.6 0.0 copy-start
  0.6 2.7 %fusion = f32[2,384]{1,0:T(2,128)S(1)} fusion(bf16[1,2,384,2048]{3,2,1,0:T(8,128)(2,1)} %param.11), kind=kLoop, calls=%fused_computation.6 | loop fusion | flops 4717824 | bytes 3148800 | tf_op jit(solution)/shard_map/reduce_sum | solution.py:167
  3.4 3.8 %fusion.11 = f32[768,2048]{1,0:T(8,128)S(1)} fusion(bf16[768,512]{1,0:T(8,128)(2,1)} %bitcast.70, bf16[1,512,2048]{2,1,0:T(8,128)(2,1)} %param.16), kind=kOutput, calls=%fused_computation.19 | convolution fusion | flops 1610612736 | bytes 9175040 | tf_op jit(solution)/shard_map/dot_general | solution.py:164
  7.2 4.9 %fusion.4 = (f32[768]{0:T(1024)S(1)}, f32[768,2048]{1,0:T(8,128)}) fusion(bf16[1,2,384,2048]{3,2,1,0:T(8,128)(2,1)S(1)} %copy-done.4, f32[2048]{0:T(1024)S(1)} %bitcast.72, f32[768,2048]{1,0:T(8,128)S(1)} %fusion.11, bf16[768,512]{1,0:T(8,128)(2,1)S(1)} %bitcast.69, bf16[1,512,2048]{2,1,0:T(8,128)(2,1)S(1)} %copy-done), kind=kOutput, calls=%fused_computation.10 | convolution fusion | flops 1618476288 | bytes 18623488 | tf_op jit(solution)/shard_map/dot_general | solution.py:164
  12.1 0.6 pad.4.x_ref
  12.7 9.0 %shard_map.138 = f32[16,128]{1,0:T(8,128)} custom-call(f32[16,128]{1,0:T(8,128)} %pad.4.x_ref), custom_call_target="tpu_custom_call" | custom-call | flops 10000 | bytes 1048576 | tf_op jit(solution)/shard_map/pallas_call | solution.py:126
  21.7 0.8 fusion.18
  22.5 0.7 add_rsqrt_fusion
  23.2 5.6 %fusion.6 = bf16[768,2048]{1,0:T(8,128)(2,1)} fusion(bf16[1,2,384,2048]{3,2,1,0:T(8,128)(2,1)} %param.11, f32[768,2048]{1,0:T(8,128)} %get-tuple-element.27, f32[768]{0:T(1024)S(1)} %fusion.18, f32[768]{0:T(1024)S(1)} %get-tuple-element.25, f32[2048]{0:T(1024)S(1)} %bitcast.73), kind=kLoop, calls=%fused_computation.12 | loop fusion | flops 9437184 | bytes 12597248 | tf_op jit(solution)/shard_map/convert_element_type | solution.py:177
  28.8 4.7 %all-to-all-start = ((bf16[4,192,2048]{2,1,0:T(8,128)(2,1)}), bf16[4,192,2048]{2,1,0:T(8,128)(2,1)}, u32[]{:S(2)}, u32[]{:S(2)}) async-start(bf16[4,192,2048]{2,1,0:T(8,128)(2,1)} %bitcast.66), calls=%async_computation | async-start | bytes 6291456 | tf_op jit(solution)/shard_map/all_to_all | solution.py:181
  33.5 4.0 %convolution_bitcast_fusion = f32[1,512,2048]{2,1,0:T(8,128)S(1)} fusion(bf16[1,2,384,2048]{3,2,1,0:T(8,128)(2,1)} %param.11, f32[2048]{0:T(1024)S(1)} %bitcast.74, f32[2,384]{1,0:T(2,128)S(1)} %sqrt.9, bf16[1,2,384,512]{3,2,1,0:T(8,128)(2,1)S(1)} %copy-done.6), kind=kOutput, calls=%fused_computation.14 | convolution fusion | flops 1616904192 | bytes 8137728 | tf_op jit(solution)/shard_map/dot_general | solution.py:138
  37.5 2.1 %convolution_bitcast_fusion.1 = f32[1,512,2048]{2,1,0:T(8,128)S(1)} fusion(bf16[1,2,384,2048]{3,2,1,0:T(8,128)(2,1)S(1)} %copy-done.5, f32[2048]{0:T(1024)S(1)} %bitcast.75, f32[2,384]{1,0:T(2,128)S(1)} %sqrt.9, bf16[1,2,384,512]{3,2,1,0:T(8,128)(2,1)S(1)} %copy-done.7), kind=kOutput, calls=%fused_computation.15 | convolution fusion | flops 1616904192 | bytes 8137728 | tf_op jit(solution)/shard_map/dot_general | solution.py:138
  39.6 5.1 %pad_maximum_fusion = (f32[2,512,2048]{2,1,0:T(8,128)}, f32[]{:T(128)}) fusion(f32[1,512,2048]{2,1,0:T(8,128)S(1)} %convolution_bitcast_fusion, f32[1,512,2048]{2,1,0:T(8,128)S(1)} %convolution_bitcast_fusion.1), kind=kLoop, calls=%fused_computation | loop fusion | flops 6291455 | bytes 16777220 | tf_op jit(solution)/shard_map/stack | solution.py:179
  44.7 1.2 %broadcast_in_dim.15.x_ref = f32[8,128]{1,0:T(8,128)} broadcast(f32[]{:T(128)} %get-tuple-element.19), dimensions={} | broadcast | bytes 4100 | tf_op jit(solution)/shard_map/broadcast_in_dim | solution.py:182
  45.9 26.0 %shard_map.139.total_ref = f32[8,128]{1,0:T(8,128)} custom-call(f32[8,128]{1,0:T(8,128)} %broadcast_in_dim.15.x_ref), custom_call_target="tpu_custom_call" | custom-call | flops 10000 | bytes 1048576 | tf_op jit(solution)/shard_map/pallas_call | solution.py:126
  71.9 3.0 %add_convert_fusion = (bf16[1,192,2048]{2,1,0:T(8,128)(2,1)S(1)}, bf16[1,192,2048]{2,1,0:T(8,128)(2,1)S(1)}, bf16[1,192,2048]{2,1,0:T(8,128)(2,1)S(1)}, bf16[1,192,2048]{2,1,0:T(8,128)(2,1)S(1)}) fusion(bf16[4,192,2048]{2,1,0:T(8,128)(2,1)} %all-to-all-done, bf16[4,192,2048]{2,1,0:T(8,128)(2,1)} %bitcast.71, s32[]{:T(128)S(6)} %select_n.4), kind=kLoop, calls=%fused_computation.21 | loop fusion | flops 5111808 | bytes 7077892 | tf_op jit(solution)/shard_map/convert_element_type | solution.py:192
  74.9 1.9 %pad_maximum_fusion.1 = bf16[4,192,2048]{2,1,0:T(8,128)(2,1)} fusion(bf16[1,192,2048]{2,1,0:T(8,128)(2,1)S(1)} %get-tuple-element.23, bf16[1,192,2048]{2,1,0:T(8,128)(2,1)S(1)} %get-tuple-element.22, bf16[1,192,2048]{2,1,0:T(8,128)(2,1)S(1)} %get-tuple-element.21, bf16[1,192,2048]{2,1,0:T(8,128)(2,1)S(1)} %get-tuple-element.20), kind=kLoop, calls=%fused_computation.17 | loop fusion | flops 4718592 | bytes 6291456 | tf_op jit(solution)/shard_map/stack | solution.py:193
  76.8 5.0 %all-to-all-start.1 = ((bf16[4,192,2048]{2,1,0:T(8,128)(2,1)}), bf16[4,192,2048]{2,1,0:T(8,128)(2,1)}, u32[]{:S(2)}, u32[]{:S(2)}) async-start(bf16[4,192,2048]{2,1,0:T(8,128)(2,1)} %pad_maximum_fusion.1), calls=%async_computation.1 | async-start | bytes 6291456 | tf_op jit(solution)/shard_map/all_to_all | solution.py:194
  81.8 0.2 copy.19
  82.0 0.2 copy.20
  82.2 3.4 %copy-done.2 = f32[2,512,2048]{2,1,0:T(8,128)S(1)} copy-done((f32[2,512,2048]{2,1,0:T(8,128)S(1)}, f32[2,512,2048]{2,1,0:T(8,128)}, u32[]{:S(2)}) %copy-start.2) | copy-done | bytes 8388632
  85.6 23.3 %shard_map.140 = (f32[2,512,2048]{2,1,0:T(8,128)}, f32[2,512,2048]{2,1,0:T(8,128)}, f32[2,512,2048]{2,1,0:T(8,128)}) custom-call(f32[8,128]{1,0:T(8,128)S(1)} %copy-done.3, f32[2,512,2048]{2,1,0:T(8,128)S(1)} %copy-done.2, s32[2,512,2048]{2,1,0:T(8,128)} %bitcast.67, s32[2,512,2048]{2,1,0:T(8,128)} %bitcast.68, f32[2,512,16]{2,1,0:T(8,128)S(1)} %bitcast.64, ...), custom_call_target="tpu_custom_call" | custom-call | flops 83886080 | bytes 50331648 | tf_op jit(solution)/shard_map/pallas_call | solution.py:60
  108.9 8.2 %all-to-all-done.1 = bf16[4,192,2048]{2,1,0:T(8,128)(2,1)} async-done(((bf16[4,192,2048]{2,1,0:T(8,128)(2,1)}), bf16[4,192,2048]{2,1,0:T(8,128)(2,1)}, u32[]{:S(2)}, u32[]{:S(2)}) %all-to-all-start.1) | async-done | bytes 3145760 | tf_op jit(solution)/shard_map/all_to_all | solution.py:194
  117.1 4.0 %copy.29 = bf16[1,2,384,2048]{3,2,1,0:T(8,128)(2,1)} copy(bf16[1,2,384,2048]{3,2,1,0:T(8,128)(2,1)} %bitcast.26) | data formatting | bytes 6291456
  (26 shorter events, 0.1 us)
Async XLA Ops:
  0.6 6.6 %copy-start = (bf16[1,512,2048]{2,1,0:T(8,128)(2,1)S(1)}, bf16[1,512,2048]{2,1,0:T(8,128)(2,1)}, u32[]{:S(2)}) copy-start(bf16[1,512,2048]{2,1,0:T(8,128)(2,1)} %param.17) | copy-start | bytes 6291460
  3.4 3.8 %copy-start.4 = (bf16[1,2,384,2048]{3,2,1,0:T(8,128)(2,1)S(1)}, bf16[1,2,384,2048]{3,2,1,0:T(8,128)(2,1)}, u32[]{:S(2)}) copy-start(bf16[1,2,384,2048]{3,2,1,0:T(8,128)(2,1)} %param.11) | copy-start | bytes 9437188
  3.4 3.8 %copy-start.6 = (bf16[1,2,384,512]{3,2,1,0:T(8,128)(2,1)S(1)}, bf16[1,2,384,512]{3,2,1,0:T(8,128)(2,1)}, u32[]{:S(2)}) copy-start(bf16[1,2,384,512]{3,2,1,0:T(8,128)(2,1)} %param.15) | copy-start | bytes 2359300
  3.4 3.8 %copy-start.8 = (f32[1,2048]{1,0:T(1,128)S(1)}, f32[1,2048]{1,0:T(1,128)}, u32[]{:S(2)}) copy-start(f32[1,2048]{1,0:T(1,128)} %param.13) | copy-start | bytes 24580
  28.8 43.1 %all-to-all-start = ((bf16[4,192,2048]{2,1,0:T(8,128)(2,1)}), bf16[4,192,2048]{2,1,0:T(8,128)(2,1)}, u32[]{:S(2)}, u32[]{:S(2)}) async-start(bf16[4,192,2048]{2,1,0:T(8,128)(2,1)} %bitcast.66), calls=%async_computation | async-start | bytes 6291456 | tf_op jit(solution)/shard_map/all_to_all | solution.py:181
  33.5 4.1 %copy-start.5 = (bf16[1,2,384,2048]{3,2,1,0:T(8,128)(2,1)S(1)}, bf16[1,2,384,2048]{3,2,1,0:T(8,128)(2,1)}, u32[]{:S(2)}) copy-start(bf16[1,2,384,2048]{3,2,1,0:T(8,128)(2,1)} %param.11) | copy-start | bytes 9437188
  33.5 4.1 %copy-start.7 = (bf16[1,2,384,512]{3,2,1,0:T(8,128)(2,1)S(1)}, bf16[1,2,384,512]{3,2,1,0:T(8,128)(2,1)}, u32[]{:S(2)}) copy-start(bf16[1,2,384,512]{3,2,1,0:T(8,128)(2,1)} %param.14) | copy-start | bytes 2359300
  76.8 5.0 %copy-start.9 = (f32[1,2,512,16]{2,3,1,0:T(8,128)S(1)}, f32[1,2,512,16]{2,3,1,0:T(8,128)}, u32[]{:S(2)}) copy-start(f32[1,2,512,16]{2,3,1,0:T(8,128)} %param.20) | copy-start | bytes 196612
  76.8 5.2 %copy-start.10 = (f32[1,2,512,16]{2,3,1,0:T(8,128)S(1)}, f32[1,2,512,16]{2,3,1,0:T(8,128)}, u32[]{:S(2)}) copy-start(f32[1,2,512,16]{2,3,1,0:T(8,128)} %param.21) | copy-start | bytes 196612
  76.8 5.4 %copy-start.3 = (f32[8,128]{1,0:T(8,128)S(1)}, f32[8,128]{1,0:T(8,128)}, u32[]{:S(2)}) copy-start(f32[8,128]{1,0:T(8,128)} %shard_map.139.total_ref) | copy-start | bytes 12292
  76.8 40.3 %all-to-all-start.1 = ((bf16[4,192,2048]{2,1,0:T(8,128)(2,1)}), bf16[4,192,2048]{2,1,0:T(8,128)(2,1)}, u32[]{:S(2)}, u32[]{:S(2)}) async-start(bf16[4,192,2048]{2,1,0:T(8,128)(2,1)} %pad_maximum_fusion.1), calls=%async_computation.1 | async-start | bytes 6291456 | tf_op jit(solution)/shard_map/all_to_all | solution.py:194
  82.2 3.4 %copy-start.2 = (f32[2,512,2048]{2,1,0:T(8,128)S(1)}, f32[2,512,2048]{2,1,0:T(8,128)}, u32[]{:S(2)}) copy-start(f32[2,512,2048]{2,1,0:T(8,128)} %get-tuple-element.18.grad_ref) | copy-start | bytes 25165828
  85.6 35.5 %copy-start.1 = (bf16[1,512,2048]{2,1,0:T(8,128)(2,1)S(1)}, bf16[1,512,2048]{2,1,0:T(8,128)(2,1)}, u32[]{:S(2)}) copy-start(bf16[1,512,2048]{2,1,0:T(8,128)(2,1)} %param.17) | copy-start | bytes 6291460
